TPU v7x, 256 devices: a whole 4x4x8 slice. The times are simulated.
256 devices in a mesh: req: 1, span: 32 (over y, x, core), head: 8 (over z).
Axes of the slice: x: 4, y: 4, z: 8, core: 2. Of those that a mesh axis runs over, the one named last changes fastest.
Arguments:
- hidden_rows: bfloat16 [32, 128, 8192], P(('req', 'span')), may hold values from -6 to 6
- w_query: bfloat16 [8192, 4096], P('span', 'head'), may hold values from -0.0625 to 0.0625
- w_key: bfloat16 [8192, 1024], P('span', 'head'), may hold values from -0.0625 to 0.0625
- w_value: bfloat16 [8192, 1024], P('span', 'head'), may hold values from -0.0625 to 0.0625
- cache_keys: bfloat16 [32, 1024, 1024], P(('req', 'span'), None, 'head'), may hold values from -4 to 4
- cache_values: bfloat16 [32, 1024, 1024], P(('req', 'span'), None, 'head'), may hold values from -4 to 4
- key_scale: float32 [32, 8, 1024], P(('req', 'span'), 'head'), may hold values from 0.5 to 240
- value_scale: float32 [32, 8, 1024], P(('req', 'span'), 'head'), may hold values from 0.5 to 2
- sel_index: int32 [32, 128], P(('req', 'span')), may hold values from 0 to 1023, as said below
- sel_count: int32 [32], P(('req', 'span')), may hold values from 64 to 128, as said below
Outputs:
- attended: bfloat16 [32, 128, 4096], P(('req', 'span'), None, 'head')
- blend_keys: bfloat16 [32, 1024, 1024], P(('req', 'span'), None, 'head')
- blend_values: bfloat16 [32, 1024, 1024], P(('req', 'span'), None, 'head')
Inputs may be any that keep to these rules, and one draw needn't show every extreme that they name: `sel_index`: within one span the 128 entries are distinct positions; only the first sel_count entries are used. `sel_count`: some span uses all 128 slots.
All inputs are finite; a program needn't handle non-finite values.
Results may differ from a plain program's by a relative error of at most 0.022.
The roundings to bfloat16 on the way count: a program that leaves them out, or rounds other values in their place, can miss the bound.
Values may be sent and summed in bfloat16 or wider, within the bound.
A program may use at most 128 MiB of HBM per device.

v0:
```python
import jax
import jax.numpy as jnp
from jax import lax
from jax.sharding import PartitionSpec as P

HEAD_DIM = 128
GROUP = 4


def attend_block(carry, queries, query_pos, keys, values, key_pos):
    best, total, accum = carry
    heads = queries.shape[1]
    key_rows = keys.reshape(keys.shape[0], heads, HEAD_DIM)
    value_rows = values.reshape(values.shape[0], heads, HEAD_DIM)
    scores = jnp.einsum(
        "rhgd,nhd->rhgn", queries, key_rows, preferred_element_type=jnp.float32
    ) * HEAD_DIM ** (-0.5)
    allowed = (key_pos[None, :] <= query_pos[:, None])[:, None, None, :]
    scores = jnp.where(allowed, scores, -1e30)
    new_best = jnp.maximum(best, jnp.max(scores, axis=-1))
    rescale = jnp.exp(best - new_best)
    weights = jnp.where(allowed, jnp.exp(scores - new_best[..., None]), 0.0)
    total = total * rescale + jnp.sum(weights, axis=-1)
    accum = accum * rescale[..., None] + jnp.einsum(
        "rhgn,nhd->rhgd",
        weights.astype(jnp.bfloat16),
        value_rows,
        preferred_element_type=jnp.float32,
    )
    return (new_best, total, accum)


def attend_spans(carry, queries, query_pos, keys, values):
    count = keys.shape[0]
    span_len = keys.shape[1]
    positions = (
        jnp.arange(count, dtype=jnp.int32)[:, None] * span_len
        + jnp.arange(span_len, dtype=jnp.int32)[None, :]
    )

    def advance(state, inputs):
        return (attend_block(state, queries, query_pos, inputs[0], inputs[1], inputs[2]), None)

    carry, _ = lax.scan(advance, carry, (keys, values, positions))
    return carry


def empty_state(rows, heads):
    return (
        jnp.full((rows, heads, GROUP), -1e30, jnp.float32),
        jnp.zeros((rows, heads, GROUP), jnp.float32),
        jnp.zeros((rows, heads, GROUP, HEAD_DIM), jnp.float32),
    )


def blend_rows(cache_rows, scale_rows, fresh_rows, target):
    span_dev, span_len, columns = cache_rows.shape
    heads = columns // HEAD_DIM
    dequantized = (
        (
            cache_rows.astype(jnp.float32).reshape(span_dev, span_len, heads, HEAD_DIM)
            * jnp.swapaxes(scale_rows, 1, 2)[..., None]
        )
        .reshape(span_dev, span_len, columns)
        .astype(jnp.bfloat16)
    )
    return jax.vmap(lambda base, where_to, rows: base.at[where_to].set(rows, mode="drop"))(
        dequantized, target, fresh_rows
    )


def shards(
    hidden_rows,
    w_query,
    w_key,
    w_value,
    cache_keys,
    cache_values,
    key_scale,
    value_scale,
    sel_index,
    sel_count,
):
    span_dev, slots, width = hidden_rows.shape
    rows = span_dev * slots
    flat = hidden_rows.reshape(rows, width)
    query_cols = w_query.shape[1]
    key_cols = w_key.shape[1]
    heads = key_cols // HEAD_DIM
    pieces = (
        lax.all_gather(w_query, "span", axis=0, tiled=True),
        lax.all_gather(w_key, "span", axis=0, tiled=True),
        lax.all_gather(w_value, "span", axis=0, tiled=True),
    )
    query_sum, key_sum, value_sum = tuple(
        (jnp.dot(flat, piece, preferred_element_type=jnp.float32) for piece in pieces)
    )
    queries = query_sum.astype(jnp.bfloat16).reshape(rows, heads, GROUP, HEAD_DIM)
    new_keys = key_sum.astype(jnp.bfloat16).reshape(span_dev, slots, key_cols)
    new_values = value_sum.astype(jnp.bfloat16).reshape(span_dev, slots, key_cols)
    span_len = cache_keys.shape[1]
    valid = jnp.arange(slots, dtype=jnp.int32)[None, :] < sel_count[:, None]
    target = jnp.where(valid, sel_index, span_len)
    blend_keys = blend_rows(cache_keys, key_scale, new_keys, target)
    blend_values = blend_rows(cache_values, value_scale, new_values, target)
    own_first = lax.axis_index("span") * span_dev
    query_pos = (
        (own_first + jnp.arange(span_dev, dtype=jnp.int32))[:, None] * span_len + sel_index
    ).reshape(rows)
    pieces = (
        lax.all_gather(blend_keys, "span", axis=0, tiled=True),
        lax.all_gather(blend_values, "span", axis=0, tiled=True),
    )
    best, total, accum = attend_spans(
        empty_state(rows, heads), queries, query_pos, pieces[0], pieces[1]
    )
    result = (accum / total[..., None]).reshape(span_dev, slots, query_cols)
    attended = jnp.where(valid[:, :, None], result, 0.0).astype(jnp.bfloat16)
    return (attended, blend_keys, blend_values)


def solution(mesh):
    placed = (
        P(("req", "span"), None, None),
        P("span", "head"),
        P("span", "head"),
        P("span", "head"),
        P(("req", "span"), None, "head"),
        P(("req", "span"), None, "head"),
        P(("req", "span"), "head", None),
        P(("req", "span"), "head", None),
        P(("req", "span"), None),
        P(("req", "span")),
    )
    return jax.shard_map(
        shards,
        mesh=mesh,
        in_specs=placed,
        out_specs=(
            P(("req", "span"), None, "head"),
            P(("req", "span"), None, "head"),
            P(("req", "span"), None, "head"),
        ),
        check_vma=False,
    )
```

profile of v0, /device:TPU:66, one launch (start us, length us, event | category | flops | bytes accessed | tf_op | source)
XLA Modules:
  0.0 522.4 jit_solution(7273634093264497756)
XLA Ops:
  12.0 49.3 %all-gather.8.cloned.1.call-done = bf16[8192,128]{1,0:T(8,128)(2,1)} async-done(((bf16[256,128]{1,0:T(8,128)(2,1)}), bf16[8192,128]{1,0:T(8,128)(2,1)}) %all-gather.8.cloned.1.call-update) | async-done | bytes 2097168 | tf_op jit(solution)/shard_map/all_gather | solution.py:92
  61.2 2.3 fusion.32
  65.6 46.3 %all-gather.12.cloned.1.call-done = bf16[8192,128]{1,0:T(8,128)(2,1)} async-done(((bf16[256,128]{1,0:T(8,128)(2,1)}), bf16[8192,128]{1,0:T(8,128)(2,1)}) %all-gather.12.cloned.1.call-update) | async-done | bytes 2097168 | tf_op jit(solution)/shard_map/all_gather | solution.py:93
  112.0 2.3 fusion.35
  116.2 56.0 %all-gather.10.cloned.1.call-done = bf16[8192,512]{1,0:T(8,128)(2,1)} async-done(((bf16[256,512]{1,0:T(8,128)(2,1)}), bf16[8192,512]{1,0:T(8,128)(2,1)}) %all-gather.10.cloned.1.call-update) | async-done | bytes 8388624 | tf_op jit(solution)/shard_map/all_gather | solution.py:91
  172.2 4.6 fusion.29
  176.9 55.9 %all-gather.14.cloned.1.call-done = bf16[32768,128]{1,0:T(8,128)(2,1)} async-done(((bf16[1024,128]{1,0:T(8,128)(2,1)}), bf16[32768,128]{1,0:T(8,128)(2,1)}) %all-gather.14.cloned.1.call-update) | async-done | bytes 8388624 | tf_op jit(solution)/shard_map/all_gather | solution.py:111
  232.8 60.6 %all-gather.16.cloned.1.call-done = bf16[32768,128]{1,0:T(8,128)(2,1)} async-done(((bf16[1024,128]{1,0:T(8,128)(2,1)}), bf16[32768,128]{1,0:T(8,128)(2,1)}) %all-gather.16.cloned.1.call-update) | async-done | bytes 8388624 | tf_op jit(solution)/shard_map/all_gather | solution.py:112
  293.3 221.6 %while.15 = (s32[]{:T(128)}, f32[128,1,4]{0,2,1:T(4,128)S(1)}, f32[128,1,4]{0,2,1:T(4,128)S(1)}, f32[128,1,4,128]{0,3,2,1:T(8,128)S(1)}, s32[32,1024]{1,0:T(8,12...) while((s32[]{:T(128)}, f32[128,1,4]{0,2,1:T(4,128)S(1)}, ...), condition=%wide.region_5.6_spmd.clone, body=%wide.region_2.5_spmd.clone.sunk | while | flops 275581952 | bytes 16429737 | solution.py:44
  293.6 2.7 fusion.53
  296.3 2.3 fusion.55
  300.5 2.7 fusion.53
  303.2 2.3 fusion.55
  307.4 2.7 fusion.53
  310.1 2.3 fusion.55
  314.3 2.7 fusion.53
  317.1 2.3 fusion.55
  321.2 2.7 fusion.53
  324.0 2.3 fusion.55
  328.2 2.7 fusion.53
  330.9 2.3 fusion.55
  335.1 2.7 fusion.53
  337.8 2.3 fusion.55
  342.0 2.7 fusion.53
  349.0 2.7 fusion.53
  355.9 2.7 fusion.53
  362.8 2.7 fusion.53
  369.7 2.7 fusion.53
  376.7 2.7 fusion.53
  383.6 2.7 fusion.53
  390.5 2.7 fusion.53
  397.4 2.7 fusion.53
  404.4 2.7 fusion.53
  411.3 2.7 fusion.53
  418.2 2.7 fusion.53
  425.1 2.7 fusion.53
  432.1 2.7 fusion.53
  439.0 2.7 fusion.53
  445.9 2.7 fusion.53
  452.8 2.7 fusion.53
  459.8 2.7 fusion.53
  466.7 2.7 fusion.53
  473.6 2.7 fusion.53
  480.6 2.7 fusion.53
  487.5 2.7 fusion.53
  494.4 2.7 fusion.53
  501.3 2.7 fusion.53
  508.3 2.7 fusion.53
  (319 shorter events, 125.7 us)
Async XLA Ops:
  7.2 54.1 %copy-start = (bf16[1,128,8192]{2,1,0:T(8,128)(2,1)S(1)}, bf16[1,128,8192]{2,1,0:T(8,128)(2,1)}, u32[]{:S(2)}) copy-start(bf16[1,128,8192]{2,1,0:T(8,128)(2,1)} %param.12) | copy-start | bytes 6291460
  7.2 54.1 %all-gather.8.cloned.1.call-start = ((), (), s32[]{:S(2)}) async-start(), calls=%async_computation | async-start | bytes 2162688 | tf_op jit(solution)/shard_map/all_gather | solution.py:92
  7.9 104.0 %all-gather.12.cloned.1.call-start = ((), (), s32[]{:S(2)}) async-start(), calls=%async_computation.2 | async-start | bytes 2162688 | tf_op jit(solution)/shard_map/all_gather | solution.py:93
  8.7 163.5 %all-gather.10.cloned.1.call-start = ((), (), s32[]{:S(2)}) async-start(), calls=%async_computation.1 | async-start | bytes 8650752 | tf_op jit(solution)/shard_map/all_gather | solution.py:91
  9.4 223.4 %all-gather.14.cloned.1.call-start = ((), (), s32[]{:S(2)}) async-start(), calls=%async_computation.3 | async-start | bytes 8650752 | tf_op jit(solution)/shard_map/all_gather | solution.py:111
  11.9 53.4 %copy-start.4 = (bf16[1,1024,128]{2,1,0:T(8,128)(2,1)S(1)}, bf16[1,1024,128]{2,1,0:T(8,128)(2,1)}, u32[]{:S(2)}) copy-start(bf16[1,1024,128]{2,1,0:T(8,128)(2,1)} %param.17) | copy-start | bytes 786436
  11.9 53.4 %copy-start.5 = (f32[1,1,1024]{2,1,0:T(1,128)S(1)}, f32[1,1,1024]{2,1,0:T(1,128)}, u32[]{:S(2)}) copy-start(f32[1,1,1024]{2,1,0:T(1,128)} %param.19) | copy-start | bytes 12292
  64.6 0.7 copy-start.3
  65.3 228.0 %all-gather.16.cloned.1.call-start = ((), (), s32[]{:S(2)}) async-start(), calls=%async_computation.4 | async-start | bytes 8650752 | tf_op jit(solution)/shard_map/all_gather | solution.py:112
  115.3 0.7 copy-start.2
  296.3 2.3 copy-start.1
  303.2 2.3 copy-start.1
  310.1 2.3 copy-start.1
  317.0 2.3 copy-start.1
  324.0 2.3 copy-start.1
  330.9 2.3 copy-start.1
  337.8 2.3 copy-start.1
  344.7 2.3 copy-start.1
  351.7 2.3 copy-start.1
  358.6 2.3 copy-start.1
  365.5 2.3 copy-start.1
  372.5 2.3 copy-start.1
  379.4 2.3 copy-start.1
  386.3 2.3 copy-start.1
  393.2 2.3 copy-start.1
  400.2 2.3 copy-start.1
  407.1 2.3 copy-start.1
  414.0 2.3 copy-start.1
  420.9 2.3 copy-start.1
  427.9 2.3 copy-start.1
  434.8 2.3 copy-start.1
  441.7 2.3 copy-start.1
  448.6 2.3 copy-start.1
  455.6 2.3 copy-start.1
  462.5 2.3 copy-start.1
  469.4 2.3 copy-start.1
  476.3 2.3 copy-start.1
  483.3 2.3 copy-start.1
  490.2 2.3 copy-start.1
  497.1 2.3 copy-start.1
  504.1 2.3 copy-start.1
  511.0 2.3 copy-start.1
Sparse Core Ops, SparseCore 0:
  10.6 50.6 all-gather.7
  63.8 48.1 all-gather.11
  114.5 57.6 all-gather.9
  175.2 57.5 all-gather.13
  235.7 57.5 all-gather.15
where the time goes:
time: 527 us; the launch traced here: 522 us
  waiting for transfers between devices  270 us (51%)
  matrix products  149 us (28%)
  other arithmetic  82.8 us (16%)
  between operations  14.6 us (3%)
    dot_general x32, matrix products, attend_block(): jnp.einsum('rhgd,nhd->rhgn', queries, key_rows, preferred_element_type=jn...  87.1 us
    reduce_sum x32, other arithmetic, attend_block(): total = total * rescale + jnp.sum(weights, axis=-1)  72.6 us
    all_gather x1, waiting for transfers between devices, shards(): lax.all_gather(blend_values, 'span', axis=0, tiled=True)  60.6 us
    all_gather x1, waiting for transfers between devices, shards(): lax.all_gather(w_query, 'span', axis=0, tiled=True)  56 us
    all_gather x1, waiting for transfers between devices, shards(): lax.all_gather(blend_keys, 'span', axis=0, tiled=True)  55.9 us
    dot_general x32, matrix products, attend_block(): jnp.einsum('rhgn,nhd->rhgd', weights.astype(jnp.bfloat16), value_rows, pr...  52.2 us
    all_gather x1, waiting for transfers between devices, shards(): lax.all_gather(w_key, 'span', axis=0, tiled=True)  49.3 us
    all_gather x1, waiting for transfers between devices, shards(): lax.all_gather(w_value, 'span', axis=0, tiled=True)  46.3 us
  transfers between devices with their start and end apart: 5, of which 5 were waited for; matrix products, arithmetic and copies ran while one was open for 3% of the time, Pallas kernels for 0%

commit v1 on v0

v1 whole, which is shorter than its diff:
```python
import math

import jax
import jax.numpy as jnp
from jax import lax
from jax.experimental import pallas as pl
from jax.experimental.pallas import tpu as pltpu
from jax.sharding import PartitionSpec as P

HEAD_DIM = 128
GROUP = 4
SLOTS = 128
SPAN_LEN = 1024
SIDE = 4
CHIPS = SIDE * SIDE
DEPTH = 256
ROWS = GROUP * SLOTS
KEYS = 2 * SPAN_LEN
EXP2_SCALE = math.log2(math.e) / math.sqrt(HEAD_DIM)
F32 = jnp.float32
BF16 = jnp.bfloat16
OFFSETS = (0, -1, 1, 2)


def position():
    span = lax.axis_index("span")
    core = lax.rem(span, 2)
    chip = lax.div(span, 2)
    return chip, core


def device_of(chip, core):
    return {"span": chip * 2 + core}


class Gather:
    def __init__(self, buf, rows, chip, core, send_sem, recv_sem):
        self.buf, self.rows, self.chip, self.core = buf, rows, chip, core
        self.send_sem, self.recv_sem = send_sem, recv_sem
        self.at = (lax.rem(chip, SIDE), lax.div(chip, SIDE))
        self.sent = []

    def block(self, dx, dy):
        x = lax.rem(self.at[0] + (dx + SIDE), SIDE)
        y = lax.rem(self.at[1] + (dy + SIDE), SIDE)
        return y * SIDE + x

    def along(self, axis, first, second):
        return self.block(first, second) if axis == 0 else self.block(second, first)

    def piece(self, half, block, kind):
        size = self.rows // 2
        start = half * size
        if kind >= 2:
            size //= 2
            start += (kind - 2) * size
        return self.buf.at[block, pl.ds(start, size), :]

    def copy(self, half, stage, j, kind, block, target):
        where = half * 20 + (kind if stage == 1 else 4 + j * 4 + kind)
        ref = self.piece(half, block, kind)
        return pltpu.make_async_remote_copy(
            src_ref=ref,
            dst_ref=ref,
            send_sem=self.send_sem.at[where],
            recv_sem=self.recv_sem.at[where],
            device_id=device_of(target, self.core),
            device_id_type=pl.DeviceIdType.MESH,
        )

    def locate(self, half, stage, j, shift):
        if stage == 1:
            return self.along(half, shift, 0)
        return self.along(half, OFFSETS[j], shift)

    def step(self, half, stage, way):
        axis = half if stage == 1 else 1 - half
        return self.along(axis, way, 0)

    def send(self, half, stage, j, kind, shift):
        way = 1 if kind % 2 == 0 else -1
        one = self.copy(half, stage, j, kind, self.locate(half, stage, j, shift), self.step(half, stage, way))
        one.start()
        self.sent.append(one)

    def receive(self, half, stage, j, kind):
        shift = (-1, 1, 2, 2)[kind]
        self.copy(half, stage, j, kind, self.locate(half, stage, j, shift), self.chip).wait_recv()

    def spread(self, half, stage, j):
        self.send(half, stage, j, 0, 0)
        self.send(half, stage, j, 1, 0)

    def begin(self):
        for half in (0, 1):
            self.spread(half, 1, 0)
        for half in (0, 1):
            self.spread(half, 2, 0)

    def fulls(self, stage, j):
        for kind in (0, 1):
            for half in (0, 1):
                self.receive(half, stage, j, kind)
                self.send(half, stage, j, kind + 2, (-1, 1)[kind])
                if stage == 1:
                    self.spread(half, 2, 1 + kind)

    def quarters(self, stage, j):
        for half in (0, 1):
            for kind in (2, 3):
                self.receive(half, stage, j, kind)
            if stage == 1:
                self.spread(half, 2, 3)

    def finish(self):
        for one in self.sent:
            one.wait_send()


def project(acc, hid_v, buf, block, first=False):
    part = jnp.dot(hid_v[block], buf[block], preferred_element_type=F32)
    acc[...] = part if first else acc[...] + part


def run_gather(gather, acc, hid_v, buf, first_work):
    def work(*pairs):
        for dx, dy in pairs:
            project(acc, hid_v, buf, gather.block(dx, dy))

    first_work()
    gather.fulls(1, 0)
    gather.fulls(2, 0)
    work((-1, 0), (1, 0), (0, -1), (0, 1))
    gather.quarters(1, 0)
    gather.fulls(2, 1)
    gather.fulls(2, 2)
    work((-1, -1), (1, -1), (-1, 1), (1, 1))
    gather.quarters(2, 0)
    work((2, 0), (0, 2))
    gather.fulls(2, 3)
    gather.quarters(2, 1)
    gather.quarters(2, 2)
    work((2, -1), (2, 1), (-1, 2), (1, 2))
    gather.quarters(2, 3)
    work((2, 2))


def body(
    hid, wq, wk, wv, ck, cv, ks, vs, sel, cnt,
    att_o, bk_o, bv_o,
    hid_v, wkv_buf, wq_buf, acc_kv, acc_q, pkv_in, pq_in, cache_v, kbuf, vbuf,
    qbuf, osend, res, stat, stat_t, stat_in, out_acc, att_v,
    local_sem, out_sem, hid_sem, part_sem, kv_sem,
    akv_send, akv_recv, aq_send, aq_recv,
    q_send, q_recv, r_send, r_recv, s_send, s_recv,
):
    chip, core = position()
    sibling = device_of(chip, 1 - core)

    def remote(src, dst, send_sem, recv_sem, device):
        return pltpu.make_async_remote_copy(
            src_ref=src, dst_ref=dst, send_sem=send_sem, recv_sem=recv_sem,
            device_id=device, device_id_type=pl.DeviceIdType.MESH,
        )

    barrier = pltpu.get_barrier_semaphore()
    pl.semaphore_signal(barrier, inc=1, device_id=sibling, device_id_type=pl.DeviceIdType.MESH)

    def greet(step, carry):
        other = lax.rem(chip + step, CHIPS)
        pl.semaphore_signal(
            barrier, inc=1, device_id=device_of(other, core), device_id_type=pl.DeviceIdType.MESH
        )
        return carry

    lax.fori_loop(1, CHIPS, greet, 0)

    loads = [
        pltpu.make_async_copy(wk, wkv_buf.at[chip, :, pl.ds(0, HEAD_DIM)], local_sem.at[0]),
        pltpu.make_async_copy(wv, wkv_buf.at[chip, :, pl.ds(HEAD_DIM, HEAD_DIM)], local_sem.at[1]),
        pltpu.make_async_copy(wq, wq_buf.at[chip], local_sem.at[2]),
        pltpu.make_async_copy(ck.at[0], cache_v.at[0], local_sem.at[3]),
        pltpu.make_async_copy(cv.at[0], cache_v.at[1], local_sem.at[4]),
    ]
    for one in loads:
        one.start()

    def load_hidden(block, carry):
        start = pl.multiple_of((block * 2 + core) * DEPTH, DEPTH)
        pltpu.make_async_copy(
            hid.at[0, :, pl.ds(start, DEPTH)], hid_v.at[block, pl.ds(0, SLOTS), :], local_sem.at[5]
        ).start()
        return carry

    lax.fori_loop(0, CHIPS, load_hidden, 0)
    pl.semaphore_wait(barrier, CHIPS)

    gkv = Gather(wkv_buf, DEPTH, chip, core, akv_send, akv_recv)
    gq = Gather(wq_buf, DEPTH, chip, core, aq_send, aq_recv)
    loads[0].wait()
    loads[1].wait()
    gkv.begin()
    loads[2].wait()
    gq.begin()

    def send_hidden(block, carry):
        start = pl.multiple_of((block * 2 + 1 - core) * DEPTH, DEPTH)
        remote(
            hid.at[0, :, pl.ds(start, DEPTH)], hid_v.at[block, pl.ds(SLOTS, SLOTS), :],
            hid_sem.at[0], hid_sem.at[1], sibling,
        ).start()
        return carry

    lax.fori_loop(0, CHIPS, send_hidden, 0)
    hid_own = hid_v.at[:, pl.ds(0, SLOTS), :]
    hid_far = hid_v.at[:, pl.ds(SLOTS, SLOTS), :]
    hid_copy = remote(hid_far, hid_far, hid_sem.at[0], hid_sem.at[1], sibling)

    loads[3].wait()
    loads[4].wait()
    own_keys = pl.multiple_of(core * SPAN_LEN, SPAN_LEN)
    for which, (scale, target) in enumerate(((ks, kbuf), (vs, vbuf))):
        for part in range(SPAN_LEN // 128):
            row = scale[0, :, part * 128:(part + 1) * 128]
            spread = jnp.transpose(jnp.broadcast_to(row, (128, 128)))
            codes = cache_v[which, part * 128:(part + 1) * 128, :].astype(F32)
            target[pl.ds(own_keys + part * 128, 128), :] = (codes * spread).astype(BF16)

    def first_kv():
        pltpu.make_async_copy(hid_own, hid_own, local_sem.at[5]).wait()
        hid_copy.wait_recv()
        project(acc_kv, hid_v, wkv_buf, chip, first=True)
        project(acc_q, hid_v, wq_buf, chip, first=True)

    run_gather(gkv, acc_kv, hid_v, wkv_buf, first_kv)
    kv_part = remote(
        acc_kv.at[pl.ds(SLOTS, SLOTS), :], pkv_in, part_sem.at[0], part_sem.at[1], sibling
    )
    kv_part.start()

    slot_row = lax.broadcasted_iota(jnp.int32, (1, SLOTS), 1)
    count = cnt[0]
    wanted = jnp.where(slot_row < count, sel[...], -1)

    def blend():
        kv_part.wait_recv()
        fresh = (acc_kv[0:SLOTS, :] + pkv_in[...]).astype(BF16)
        ones = jnp.ones((SLOTS, HEAD_DIM), BF16)

        def part(step, carry):
            start = pl.multiple_of(step * 128, 128)
            rows = lax.broadcasted_iota(jnp.int32, (128, SLOTS), 0) + start
            chosen = jnp.where(rows == wanted, 1.0, 0.0).astype(BF16)
            moved = jnp.dot(chosen, fresh, preferred_element_type=F32)
            hit = jnp.dot(chosen, ones, preferred_element_type=F32) > 0.5
            here = pl.ds(pl.multiple_of(own_keys + start, 128), 128)
            kbuf[here, :] = jnp.where(hit, moved[:, :HEAD_DIM], kbuf[here, :].astype(F32)).astype(BF16)
            vbuf[here, :] = jnp.where(hit, moved[:, HEAD_DIM:], vbuf[here, :].astype(F32)).astype(BF16)
            return carry

        lax.fori_loop(0, SPAN_LEN // 128, part, 0)

    own_span = pl.ds(own_keys, SPAN_LEN)
    k_copy = remote(kbuf.at[own_span, :], kbuf.at[own_span, :], kv_sem.at[0], kv_sem.at[1], sibling)
    v_copy = remote(vbuf.at[own_span, :], vbuf.at[own_span, :], kv_sem.at[2], kv_sem.at[3], sibling)
    k_out = pltpu.make_async_copy(kbuf.at[own_span, :], bk_o.at[0], out_sem.at[0])
    v_out = pltpu.make_async_copy(vbuf.at[own_span, :], bv_o.at[0], out_sem.at[1])

    def start_kv():
        blend()
        for one in (k_copy, v_copy, k_out, v_out):
            one.start()

    run_gather(gq, acc_q, hid_v, wq_buf, start_kv)
    q_part = remote(acc_q.at[pl.ds(SLOTS, SLOTS), :], pq_in, part_sem.at[2], part_sem.at[3], sibling)
    q_part.start()
    other_keys = pl.multiple_of((1 - core) * SPAN_LEN, SPAN_LEN)
    other_span = pl.ds(other_keys, SPAN_LEN)
    remote(kbuf.at[other_span, :], kbuf.at[other_span, :], kv_sem.at[0], kv_sem.at[1], sibling).wait_recv()
    remote(vbuf.at[other_span, :], vbuf.at[other_span, :], kv_sem.at[2], kv_sem.at[3], sibling).wait_recv()
    stat[...] = jnp.zeros((ROWS, 128), F32)
    q_part.wait_recv()
    for g in range(GROUP):
        cols = slice(g * HEAD_DIM, (g + 1) * HEAD_DIM)
        qbuf[chip, cols, :] = (acc_q[0:SLOTS, cols] + pq_in[:, cols]).astype(BF16)

    def q_copy(source, target):
        return remote(
            qbuf.at[source], qbuf.at[source], q_send.at[target], q_recv.at[source],
            device_of(target, core),
        )

    def send_q(target, carry):
        q_copy(chip, target).start()
        return carry

    lax.fori_loop(0, chip, send_q, 0)

    lane = lax.broadcasted_iota(jnp.int32, (256, 128), 1)

    def attend(source, half, store, limit):
        here = pl.ds(pl.multiple_of(half * 256, 256), 256)
        scores = lax.dot_general(
            qbuf[source, here, :], kbuf[...], (((1,), (1,)), ((), ())), preferred_element_type=F32
        )
        if limit is not None:
            key = lax.broadcasted_iota(jnp.int32, (256, KEYS), 1)
            scores = jnp.where(key <= limit, scores, -1e30)
        best = jnp.max(scores, axis=1, keepdims=True)
        weights = jnp.exp2((scores - best) * EXP2_SCALE)
        total = jnp.sum(weights, axis=1, keepdims=True)
        summed = jnp.dot(weights.astype(BF16), vbuf[...], preferred_element_type=F32)
        store[source, here, :] = summed.astype(BF16)
        old = stat[here, :]
        old = jnp.where(lane == source * 8, best, old)
        stat[here, :] = jnp.where(lane == source * 8 + 1, total, old)

    place = jnp.transpose(jnp.broadcast_to(sel[...], (128, 128)))[:, 0:1] + core * SPAN_LEN
    limit = jnp.concatenate([place, place], axis=0)

    def own_half(half, carry):
        attend(chip, half, res, limit)
        return carry

    lax.fori_loop(0, 2, own_half, 0)

    def r_copy(source, target):
        return remote(
            osend.at[target], res.at[source], r_send.at[target], r_recv.at[source],
            device_of(target, core),
        )

    def s_copy(source, target):
        return remote(
            stat_t.at[target], stat_in.at[source], s_send.at[target], s_recv.at[source],
            device_of(target, core),
        )

    def others(source, carry):
        q_copy(source, chip).wait_recv()

        def one_half(half, inner):
            attend(source, half, osend, None)
            return inner

        lax.fori_loop(0, 2, one_half, 0)
        r_copy(chip, source).start()
        return carry

    lax.fori_loop(chip + 1, CHIPS, others, 0)
    stat_t[...] = jnp.transpose(stat[...]).reshape(CHIPS, 8, ROWS)

    def send_stat(target, carry):
        s_copy(chip, target).start()
        return carry

    lax.fori_loop(chip + 1, CHIPS, send_stat, 0)
    stat_in[chip] = stat_t[chip]

    def take(source, carry):
        s_copy(source, chip).wait_recv()
        return carry

    lax.fori_loop(0, chip, take, 0)
    seen = stat_in[...]
    known = lax.broadcasted_iota(jnp.int32, (CHIPS, 1, ROWS), 0) <= chip
    bests = jnp.where(known, seen[:, 0:1, :], -3e38)
    top = jnp.max(bests, axis=0, keepdims=True)
    factor = jnp.where(known, jnp.exp2((bests - top) * EXP2_SCALE), 0.0)
    total = jnp.sum(jnp.where(known, factor * seen[:, 1:2, :], 0.0), axis=0, keepdims=True)
    factor = factor / total
    stat[...] = jnp.transpose(jnp.broadcast_to(factor, (CHIPS, 8, ROWS)).reshape(CHIPS * 8, ROWS))
    out_acc[...] = jnp.zeros((ROWS, HEAD_DIM), F32)

    def add(source):
        wide = lax.broadcasted_iota(jnp.int32, (ROWS, 128), 1)
        weight = jnp.sum(jnp.where(wide == source * 8, stat[...], 0.0), axis=1, keepdims=True)
        out_acc[...] += res[source].astype(F32) * weight

    add(chip)

    def add_far(source, carry):
        r_copy(source, chip).wait_recv()
        add(source)
        return carry

    lax.fori_loop(0, chip, add_far, 0)
    used = lax.broadcasted_iota(jnp.int32, (SLOTS, HEAD_DIM), 0) < count
    for g in range(GROUP):
        cols = slice(g * HEAD_DIM, (g + 1) * HEAD_DIM)
        att_v[:, cols] = jnp.where(used, out_acc[cols, :], 0.0).astype(BF16)
    a_out = pltpu.make_async_copy(att_v, att_o.at[0], out_sem.at[2])
    a_out.start()

    gkv.finish()
    gq.finish()
    hid_copy.wait_send()
    kv_part.wait_send()
    q_part.wait_send()
    k_copy.wait_send()
    v_copy.wait_send()

    def end_q(target, carry):
        q_copy(chip, target).wait_send()
        return carry

    def end_r(target, carry):
        r_copy(chip, target).wait_send()
        s_copy(chip, target).wait_send()
        return carry

    lax.fori_loop(0, chip, end_q, 0)
    lax.fori_loop(chip + 1, CHIPS, end_r, 0)
    for one in (k_out, v_out, a_out):
        one.wait()


def shards(hidden_rows, w_query, w_key, w_value, cache_keys, cache_values, key_scale, value_scale, sel_index, sel_count):
    any_spec = pl.BlockSpec(memory_space=pl.ANY)
    vmem_spec = pl.BlockSpec(memory_space=pltpu.VMEM)
    smem_spec = pl.BlockSpec(memory_space=pltpu.SMEM)
    dma = pltpu.SemaphoreType.DMA
    return pl.pallas_call(
        body,
        out_shape=(
            jax.ShapeDtypeStruct((1, SLOTS, ROWS), BF16),
            jax.ShapeDtypeStruct((1, SPAN_LEN, HEAD_DIM), BF16),
            jax.ShapeDtypeStruct((1, SPAN_LEN, HEAD_DIM), BF16),
        ),
        in_specs=[any_spec] * 6 + [vmem_spec] * 3 + [smem_spec],
        out_specs=(any_spec,) * 3,
        scratch_shapes=[
            pltpu.VMEM((CHIPS, 2 * SLOTS, DEPTH), BF16),
            pltpu.VMEM((CHIPS, DEPTH, 2 * HEAD_DIM), BF16),
            pltpu.VMEM((CHIPS, DEPTH, ROWS), BF16),
            pltpu.VMEM((2 * SLOTS, 2 * HEAD_DIM), F32),
            pltpu.VMEM((2 * SLOTS, ROWS), F32),
            pltpu.VMEM((SLOTS, 2 * HEAD_DIM), F32),
            pltpu.VMEM((SLOTS, ROWS), F32),
            pltpu.VMEM((2, SPAN_LEN, HEAD_DIM), BF16),
            pltpu.VMEM((KEYS, HEAD_DIM), BF16),
            pltpu.VMEM((KEYS, HEAD_DIM), BF16),
            pltpu.VMEM((CHIPS, ROWS, HEAD_DIM), BF16),
            pltpu.VMEM((CHIPS, ROWS, HEAD_DIM), BF16),
            pltpu.VMEM((CHIPS, ROWS, HEAD_DIM), BF16),
            pltpu.VMEM((ROWS, 128), F32),
            pltpu.VMEM((CHIPS, 8, ROWS), F32),
            pltpu.VMEM((CHIPS, 8, ROWS), F32),
            pltpu.VMEM((ROWS, HEAD_DIM), F32),
            pltpu.VMEM((SLOTS, ROWS), BF16),
            dma((6,)), dma((3,)), dma((2,)), dma((4,)), dma((4,)),
            dma((40,)), dma((40,)), dma((40,)), dma((40,)),
            dma((CHIPS,)), dma((CHIPS,)), dma((CHIPS,)), dma((CHIPS,)), dma((CHIPS,)), dma((CHIPS,)),
        ],
        compiler_params=pltpu.CompilerParams(
            collective_id=0, has_side_effects=True, vmem_limit_bytes=48 * 1024 * 1024
        ),
        name="span_attention",
    )(hidden_rows, w_query, w_key, w_value, cache_keys, cache_values, key_scale, value_scale, sel_index, sel_count)


def solution(mesh):
    placed = (
        P(("req", "span"), None, None),
        P("span", "head"),
        P("span", "head"),
        P("span", "head"),
        P(("req", "span"), None, "head"),
        P(("req", "span"), None, "head"),
        P(("req", "span"), "head", None),
        P(("req", "span"), "head", None),
        P(("req", "span"), None),
        P(("req", "span")),
    )
    return jax.shard_map(
        shards,
        mesh=mesh,
        in_specs=placed,
        out_specs=(
            P(("req", "span"), None, "head"),
            P(("req", "span"), None, "head"),
            P(("req", "span"), None, "head"),
        ),
        check_vma=False,
    )
```

time: 527 us -> 128 us (0.24)
  the two profiles are of different devices: /device:TPU:66 before, /device:TPU:63 now
where the time goes in v1:
time: 128 us; the launch traced here: 127 us
  Pallas kernels  116 us (91%)
  local copies, waits for them, and re-layouts  10.2 us (8%)
  between operations  1.31 us (1%)
    pallas_call x1, Pallas kernels, shards(): pl.pallas_call(body, out_shape=(jax.ShapeDtypeStruct((1, SLOTS, ROWS), BF...  116 us
    unnamed x21, local copies, waits for them, and re-layouts  10.2 us

profile of v1, /device:TPU:63, one launch (start us, length us, event | category | flops | bytes accessed | tf_op | source)
XLA Modules:
  0.0 127.4 jit_solution(8585095626145488638)
XLA Ops:
  1.3 0.0 copy-start
  1.3 1.6 %copy-done = bf16[1,128,8192]{2,1,0:T(8,128)(2,1)S(1)} copy-done((bf16[1,128,8192]{2,1,0:T(8,128)(2,1)S(1)}, bf16[1,128,8192]{2,1,0:T(8,128)(2,1)}, u32[]{:S(2)}) %copy-start) | copy-done | bytes 2097176
  2.9 0.0 copy-start.1
  2.9 0.9 copy-done.1
  3.8 0.0 copy-start.2
  3.8 0.9 copy-done.2
  4.8 0.0 copy-start.3
  4.8 0.9 copy-done.3
  5.7 0.0 copy-start.4
  5.7 0.8 copy-done.4
  6.6 0.0 copy-start.5
  6.6 0.8 copy-done.5
  7.4 0.0 copy-start.6
  7.4 0.7 copy-done.6
  8.1 0.0 copy-start.7
  8.1 0.7 copy-done.7
  8.8 0.0 copy-start.8
  8.8 0.7 copy-done.8
  9.4 115.9 %span_attention.1 = (bf16[1,128,512]{2,1,0:T(8,128)(2,1)S(1)}, bf16[1,1024,128]{2,1,0:T(8,128)(2,1)S(1)}, bf16[1,1024,128]{2,1,0:T(8,128)(2,1)S(1)}) custom-call(bf16[1,128,8192]{2,1,0:T(8,128)(2,1)S(1)} %copy-done, bf16[256,512]{1,0:T(8,128)(2,1)S(1)} %copy-done.1, bf16[256,128]{1,0:T(8,128)(2,1)S(1)} %copy-done.4, bf16[256,128]{1,0:T(8,128)(2,1)S(1)} %copy-done.5, ...), custom_call_target="tpu_custom_call" | custom-call | tf_op jit(solution)/shard_map/span_attention/pallas_call | solution.py:423
  125.3 0.7 copy.17
  126.0 0.7 copy.18
  126.7 0.7 copy.19
Async XLA Ops:
  1.3 1.6 %copy-start = (bf16[1,128,8192]{2,1,0:T(8,128)(2,1)S(1)}, bf16[1,128,8192]{2,1,0:T(8,128)(2,1)}, u32[]{:S(2)}) copy-start(bf16[1,128,8192]{2,1,0:T(8,128)(2,1)} %hid.1) | copy-start | bytes 6291460
  2.9 0.9 copy-start.1
  3.8 0.9 copy-start.2
  4.8 0.9 copy-start.3
  5.7 0.8 copy-start.4
  6.6 0.8 copy-start.5
  7.4 0.7 copy-start.6
  8.1 0.7 copy-start.7
  8.8 0.7 copy-start.8

commit v2 on v1

v2 whole, which is shorter than its diff:
```python
import math

import jax
import jax.numpy as jnp
from jax import lax
from jax.experimental import pallas as pl
from jax.experimental.pallas import tpu as pltpu
from jax.sharding import PartitionSpec as P

HEAD_DIM = 128
GROUP = 4
SLOTS = 128
SPAN_LEN = 1024
SIDE = 4
CHIPS = SIDE * SIDE
DEPTH = 256
ROWS = GROUP * SLOTS
KEYS = 2 * SPAN_LEN
EXP2_SCALE = math.log2(math.e) / math.sqrt(HEAD_DIM)
F32 = jnp.float32
BF16 = jnp.bfloat16
OFFSETS = (0, -1, 1, 2)


def position():
    span = lax.axis_index("span")
    core = lax.rem(span, 2)
    chip = lax.div(span, 2)
    return chip, core


def device_of(chip, core):
    return {"span": chip * 2 + core}


class Gather:
    def __init__(self, buf, first, rows, chip, core, send_sem, recv_sem):
        self.buf, self.first, self.rows, self.chip, self.core = buf, first, rows, chip, core
        self.send_sem, self.recv_sem = send_sem, recv_sem
        self.at = (lax.rem(chip, SIDE), lax.div(chip, SIDE))
        self.sent = []

    def block(self, dx, dy):
        x = lax.rem(self.at[0] + (dx + SIDE), SIDE)
        y = lax.rem(self.at[1] + (dy + SIDE), SIDE)
        return y * SIDE + x

    def along(self, axis, first, second):
        return self.block(first, second) if axis == 0 else self.block(second, first)

    def piece(self, half, block, kind):
        size = self.first if half == 0 else self.rows - self.first
        start = half * self.first
        if kind >= 2:
            size //= 2
            start += (kind - 2) * size
        return self.buf.at[block, pl.ds(start, size), :]

    def copy(self, half, stage, j, kind, block, target):
        where = half * 20 + (kind if stage == 1 else 4 + j * 4 + kind)
        ref = self.piece(half, block, kind)
        return pltpu.make_async_remote_copy(
            src_ref=ref,
            dst_ref=ref,
            send_sem=self.send_sem.at[where],
            recv_sem=self.recv_sem.at[where],
            device_id=device_of(target, self.core),
            device_id_type=pl.DeviceIdType.MESH,
        )

    def locate(self, half, stage, j, shift):
        if stage == 1:
            return self.along(half, shift, 0)
        return self.along(half, OFFSETS[j], shift)

    def step(self, half, stage, way):
        axis = half if stage == 1 else 1 - half
        return self.along(axis, way, 0)

    def send(self, half, stage, j, kind, shift):
        way = 1 if kind % 2 == 0 else -1
        one = self.copy(half, stage, j, kind, self.locate(half, stage, j, shift), self.step(half, stage, way))
        one.start()
        self.sent.append(one)

    def receive(self, half, stage, j, kind):
        shift = (-1, 1, 2, 2)[kind]
        self.copy(half, stage, j, kind, self.locate(half, stage, j, shift), self.chip).wait_recv()

    def spread(self, half, stage, j):
        self.send(half, stage, j, 0, 0)
        self.send(half, stage, j, 1, 0)

    def begin(self):
        for half in (0, 1):
            self.spread(half, 1, 0)
        for half in (0, 1):
            self.spread(half, 2, 0)

    def fulls(self, stage, j):
        for kind in (0, 1):
            for half in (0, 1):
                self.receive(half, stage, j, kind)
                self.send(half, stage, j, kind + 2, (-1, 1)[kind])
                if stage == 1:
                    self.spread(half, 2, 1 + kind)

    def quarters(self, stage, j):
        for half in (0, 1):
            for kind in (2, 3):
                self.receive(half, stage, j, kind)
            if stage == 1:
                self.spread(half, 2, 3)

    def finish(self):
        for one in self.sent:
            one.wait_send()


class Ring:
    def __init__(self, refs, whole, at, device, send_sem, recv_sem):
        self.refs, self.whole, self.at, self.device = refs, whole, at, device
        self.send_sem, self.recv_sem = send_sem, recv_sem
        self.sent = []

    def place(self, shift):
        return lax.rem(self.at + (shift + SIDE), SIDE)

    def copy(self, kind, shift, way):
        block = self.place(shift)
        ref = self.whole(block) if kind < 2 else self.refs(block, kind - 2)
        return pltpu.make_async_remote_copy(
            src_ref=ref,
            dst_ref=ref,
            send_sem=self.send_sem.at[kind],
            recv_sem=self.recv_sem.at[kind],
            device_id=self.device(self.place(way)),
            device_id_type=pl.DeviceIdType.MESH,
        )

    def send(self, kind, shift):
        one = self.copy(kind, shift, 1 if kind % 2 == 0 else -1)
        one.start()
        self.sent.append(one)

    def begin(self):
        self.send(0, 0)
        self.send(1, 0)

    def full(self, kind):
        shift = (-1, 1)[kind]
        self.copy(kind, shift, 1).wait_recv()
        self.send(kind + 2, shift)

    def halves(self):
        self.copy(2, 2, 1).wait_recv()
        self.copy(3, 2, 1).wait_recv()

    def finish(self):
        for one in self.sent:
            one.wait_send()


def project(acc, hid_v, buf, block, first=False):
    part = jnp.dot(hid_v[block], buf[block], preferred_element_type=F32)
    acc[...] = part if first else acc[...] + part


def run_gather(gather, acc, hid_v, buf, first_work, late_work, last_work):
    def work(*pairs):
        for dx, dy in pairs:
            project(acc, hid_v, buf, gather.block(dx, dy))

    first_work()
    gather.fulls(1, 0)
    gather.fulls(2, 0)
    work((-1, 0), (1, 0), (0, -1), (0, 1))
    gather.quarters(1, 0)
    gather.fulls(2, 1)
    gather.fulls(2, 2)
    work((-1, -1), (1, -1), (-1, 1), (1, 1))
    gather.quarters(2, 0)
    work((2, 0), (0, 2))
    late_work()
    gather.fulls(2, 3)
    gather.quarters(2, 1)
    gather.quarters(2, 2)
    work((2, -1), (2, 1), (-1, 2), (1, 2))
    gather.quarters(2, 3)
    last_work()
    work((2, 2))


def body(
    hid, wq, wk, wv, ck, cv, ks_h, vs_h, sel_h, cnt_h,
    att_o, bk_o, bv_o,
    hid_v, wkv_buf, wq_buf, acc_kv, acc_q, pkv_in, pq_in, cache_v, kv,
    ks, vs, sel, cnt, q_stage, qbuf, peak, mass, accum,
    r_out, r_in, s_out, s_in, fin, att_in,
    local_sem, out_sem, hid_sem, part_sem, sib_send, sib_recv,
    akv_send, akv_recv, aq_send, aq_recv, ring_kv_send, ring_kv_recv, ring_q_send, ring_q_recv,
    sel_send, sel_recv, qy_send, qy_recv, r_send, r_recv, s_send, s_recv, f_send, f_recv,
):
    chip, core = position()
    at_x, at_y = lax.rem(chip, SIDE), lax.div(chip, SIDE)
    sibling = device_of(chip, 1 - core)

    def in_row(x):
        return device_of(at_y * SIDE + x, core)

    def in_column(y):
        return device_of(y * SIDE + at_x, core)

    def remote(src, dst, send_sem, recv_sem, device):
        return pltpu.make_async_remote_copy(
            src_ref=src, dst_ref=dst, send_sem=send_sem, recv_sem=recv_sem,
            device_id=device, device_id_type=pl.DeviceIdType.MESH,
        )

    barrier = pltpu.get_barrier_semaphore()

    def greet(device):
        pl.semaphore_signal(barrier, inc=1, device_id=device, device_id_type=pl.DeviceIdType.MESH)

    greet(sibling)
    for step in (1, 2, 3):
        greet(in_row(lax.rem(at_x + step, SIDE)))
        greet(in_column(lax.rem(at_y + step, SIDE)))

    loads = [
        pltpu.make_async_copy(wk, wkv_buf.at[chip, :, pl.ds(0, HEAD_DIM)], local_sem.at[0]),
        pltpu.make_async_copy(wv, wkv_buf.at[chip, :, pl.ds(HEAD_DIM, HEAD_DIM)], local_sem.at[1]),
        pltpu.make_async_copy(wq, wq_buf.at[chip], local_sem.at[2]),
        pltpu.make_async_copy(ck.at[0], cache_v.at[0], local_sem.at[3]),
        pltpu.make_async_copy(cv.at[0], cache_v.at[1], local_sem.at[4]),
        pltpu.make_async_copy(ks_h, ks, local_sem.at[6]),
        pltpu.make_async_copy(vs_h, vs, local_sem.at[7]),
        pltpu.make_async_copy(sel_h, sel.at[at_y], local_sem.at[8]),
        pltpu.make_async_copy(cnt_h, cnt, local_sem.at[9]),
    ]
    for one in loads:
        one.start()

    def load_hidden(block, carry):
        start = pl.multiple_of((block * 2 + core) * DEPTH, DEPTH)
        pltpu.make_async_copy(
            hid.at[0, :, pl.ds(start, DEPTH)], hid_v.at[block, pl.ds(0, SLOTS), :], local_sem.at[5]
        ).start()
        return carry

    lax.fori_loop(0, CHIPS, load_hidden, 0)
    pl.semaphore_wait(barrier, 7)

    gkv = Gather(wkv_buf, DEPTH // 2, DEPTH, chip, core, akv_send, akv_recv)
    gq = Gather(wq_buf, DEPTH // 4, DEPTH, chip, core, aq_send, aq_recv)
    loads[0].wait()
    loads[1].wait()
    gkv.begin()
    loads[2].wait()
    gq.begin()

    def send_hidden(block, carry):
        start = pl.multiple_of((block * 2 + 1 - core) * DEPTH, DEPTH)
        remote(
            hid.at[0, :, pl.ds(start, DEPTH)], hid_v.at[block, pl.ds(SLOTS, SLOTS), :],
            hid_sem.at[0], hid_sem.at[1], sibling,
        ).start()
        return carry

    lax.fori_loop(0, CHIPS, send_hidden, 0)
    hid_own = hid_v.at[:, pl.ds(0, SLOTS), :]
    hid_far = hid_v.at[:, pl.ds(SLOTS, SLOTS), :]
    hid_copy = remote(hid_far, hid_far, hid_sem.at[0], hid_sem.at[1], sibling)

    for one in loads[3:]:
        one.wait()

    def column_copy(src, dst, sends, recvs, step, back):
        slot = step - 1
        other = lax.rem(at_y + (SIDE - step if back else step), SIDE)
        return remote(src(other), dst(other if back else at_y), sends.at[slot], recvs.at[slot], in_column(other))

    def sel_copy(step, back):
        return column_copy(
            lambda other: sel.at[other if back else at_y], lambda row: sel.at[row],
            sel_send, sel_recv, step, back,
        )

    for step in (1, 2, 3):
        sel_copy(step, False).start()

    for which, scale in enumerate((ks, vs)):
        for part in range(SPAN_LEN // 128):
            rows = slice(part * 128, (part + 1) * 128)
            spread = jnp.transpose(jnp.broadcast_to(scale[0, :, rows], (128, 128)))
            kv[at_y, which, core, rows, :] = (cache_v[which, rows, :].astype(F32) * spread).astype(BF16)

    def first_kv():
        pltpu.make_async_copy(hid_own, hid_own, local_sem.at[5]).wait()
        hid_copy.wait_recv()
        project(acc_kv, hid_v, wkv_buf, chip, first=True)
        project(acc_q, hid_v, wq_buf, chip, first=True)

    run_gather(gkv, acc_kv, hid_v, wkv_buf, first_kv, lambda: None, lambda: None)
    kv_part = remote(
        acc_kv.at[pl.ds(SLOTS, SLOTS), :], pkv_in, part_sem.at[0], part_sem.at[1], sibling
    )
    kv_part.start()
    count = cnt[0]
    slot_row = lax.broadcasted_iota(jnp.int32, (1, SLOTS), 1)
    wanted = jnp.where(slot_row < count, sel[at_y], -1)

    ring_kv = Ring(
        lambda row, which: kv.at[row, which, core], lambda row: kv.at[row, :, core],
        at_y, in_column, ring_kv_send, ring_kv_recv,
    )
    ring_q = Ring(
        lambda x, which: qbuf.at[x, pl.ds(which * 2, 2)], lambda x: qbuf.at[x],
        at_x, in_row, ring_q_send, ring_q_recv,
    )

    def to_sibling(shift, owner):
        block = ring_kv.place(shift)
        ref = kv.at[block, :, owner]
        return remote(ref, ref, sib_send.at[shift + 1], sib_recv.at[shift + 1], sibling)

    k_out = pltpu.make_async_copy(kv.at[at_y, 0, core], bk_o.at[0], out_sem.at[0])
    v_out = pltpu.make_async_copy(kv.at[at_y, 1, core], bv_o.at[0], out_sem.at[1])

    def blend():
        kv_part.wait_recv()
        fresh = (acc_kv[0:SLOTS, :] + pkv_in[...]).astype(BF16)
        ones = jnp.ones((SLOTS, HEAD_DIM), BF16)

        def part(step, carry):
            start = pl.multiple_of(step * 128, 128)
            rows = lax.broadcasted_iota(jnp.int32, (128, SLOTS), 0) + start
            chosen = jnp.where(rows == wanted, 1.0, 0.0).astype(BF16)
            moved = jnp.dot(chosen, fresh, preferred_element_type=F32)
            hit = jnp.dot(chosen, ones, preferred_element_type=F32) > 0.5
            for which in (0, 1):
                new = moved[:, which * HEAD_DIM:(which + 1) * HEAD_DIM]
                old = kv[at_y, which, core, pl.ds(start, 128), :].astype(F32)
                kv[at_y, which, core, pl.ds(start, 128), :] = jnp.where(hit, new, old).astype(BF16)
            return carry

        lax.fori_loop(0, SPAN_LEN // 128, part, 0)
        ring_kv.begin()
        to_sibling(0, core).start()
        k_out.start()
        v_out.start()

    def pass_kv():
        for kind, shift in ((0, -1), (1, 1)):
            ring_kv.full(kind)
            to_sibling(shift, core).start()

    def end_kv():
        ring_kv.halves()
        to_sibling(2, core).start()

    run_gather(gq, acc_q, hid_v, wq_buf, blend, pass_kv, end_kv)
    q_part = remote(acc_q.at[pl.ds(SLOTS, SLOTS), :], pq_in, part_sem.at[2], part_sem.at[3], sibling)
    q_part.start()
    peak[...] = jnp.full((SIDE, ROWS, 128), -1e30, F32)
    mass[...] = jnp.zeros((SIDE, ROWS, 128), F32)
    accum[...] = jnp.zeros((SIDE, ROWS, HEAD_DIM), F32)
    q_part.wait_recv()
    for g in range(GROUP):
        cols = slice(g * HEAD_DIM, (g + 1) * HEAD_DIM)
        q_stage[g] = (acc_q[0:SLOTS, cols] + pq_in[:, cols]).astype(BF16)

    def qy_copy(step, back):
        return column_copy(
            lambda other: q_stage.at[other], lambda row: qbuf.at[at_x, row], qy_send, qy_recv, step, back
        )

    for step in (1, 2, 3):
        qy_copy(step, False).start()
    qbuf[at_x, at_y] = q_stage[at_y]
    for shift in (0, -1, 1, 2):
        to_sibling(shift, 1 - core).wait_recv()
    for step in (1, 2, 3):
        qy_copy(step, True).wait_recv()
        sel_copy(step, True).wait_recv()
    ring_q.begin()

    def scored(x, row, block):
        keys = kv[block, 0].reshape(KEYS, HEAD_DIM)
        return lax.dot_general(
            qbuf[x, row], keys, (((1,), (1,)), ((), ())), preferred_element_type=F32
        )

    def attend(x, pairs, masked):
        ahead = scored(x, *pairs[0])
        for index, (row, block) in enumerate(pairs):
            here = slice(row * SLOTS, (row + 1) * SLOTS)
            scores = ahead
            if index + 1 < len(pairs):
                ahead = scored(x, *pairs[index + 1])
            if masked:
                key = lax.broadcasted_iota(jnp.int32, (SLOTS, KEYS), 1)
                place = jnp.transpose(jnp.broadcast_to(sel[row], (128, 128)))[:, 0:1] + core * SPAN_LEN
                scores = jnp.where(key <= place, scores, -1e30)
            before = peak[x, here, :]
            best = jnp.maximum(before, jnp.max(scores, axis=1, keepdims=True))
            fade = jnp.exp2((before - best) * EXP2_SCALE)
            weights = jnp.exp2((scores - best[:, 0:1]) * EXP2_SCALE)
            peak[x, here, :] = best
            mass[x, here, :] = mass[x, here, :] * fade + jnp.sum(weights, axis=1, keepdims=True)
            accum[x, here, :] = accum[x, here, :] * fade + jnp.dot(
                weights.astype(BF16), kv[block, 1].reshape(KEYS, HEAD_DIM), preferred_element_type=F32
            )

    earlier = [(1, 0), (2, 0), (3, 0), (2, 1), (3, 1), (3, 2)]
    level = [(0, 0), (1, 1), (2, 2), (3, 3)]

    def r_copy(step, back):
        slot = step - 1
        other = lax.rem(at_x + (SIDE - step if back else step), SIDE)
        return (
            remote(
                r_out.at[other], r_in.at[other if back else at_x],
                r_send.at[slot], r_recv.at[slot], in_row(other),
            ),
            remote(
                s_out.at[other], s_in.at[other if back else at_x],
                s_send.at[slot], s_recv.at[slot], in_row(other),
            ),
        )

    def stats(x):
        lane = lax.broadcasted_iota(jnp.int32, (ROWS, 128), 1)
        both = jnp.where(lane == 0, peak[x], mass[x])
        return jnp.transpose(both)[0:8, :]

    def one_chip(index, carry):
        step = jnp.where(index == 0, 0, jnp.where(index == 1, 3, jnp.where(index == 2, 1, 2)))
        x = lax.rem(at_x + step, SIDE)

        @pl.when(index == 1)
        def _():
            ring_q.full(0)

        @pl.when(index == 2)
        def _():
            ring_q.full(1)

        @pl.when(index == 3)
        def _():
            ring_q.halves()

        attend(x, earlier, False)

        @pl.when(x > at_x)
        def _():
            attend(x, level, False)

        @pl.when(index > 0)
        def _():
            r_out[x] = accum[x].astype(BF16)
            s_out[x] = stats(x)

        for which, way in ((1, 3), (2, 1), (3, 2)):
            @pl.when(index == which)
            def _(way=way):
                for one in r_copy(way, False):
                    one.start()

        return carry

    lax.fori_loop(0, SIDE, one_chip, 0)
    attend(at_x, level, True)
    s_in[at_x] = stats(at_x)
    for step in (1, 3, 2):
        for one in r_copy(step, True):
            one.wait_recv()
    seen = s_in[...]
    bests = seen[:, 0:1, :]
    top = jnp.max(bests, axis=0, keepdims=True)
    factor = jnp.exp2((bests - top) * EXP2_SCALE)
    total = jnp.sum(factor * seen[:, 1:2, :], axis=0, keepdims=True)
    factor = jnp.broadcast_to(factor / total, (SIDE, 32, ROWS)).reshape(SIDE * 32, ROWS)
    factor = jnp.transpose(factor)
    r_in[at_x] = accum[at_x].astype(BF16)
    merged = jnp.zeros((ROWS, HEAD_DIM), F32)
    for x in range(SIDE):
        merged += r_in[x].astype(F32) * factor[:, x * 32:x * 32 + 1]
    fin[...] = merged.reshape(SIDE, SLOTS, HEAD_DIM).astype(BF16)

    def f_copy(step, back):
        return column_copy(
            lambda other: fin.at[other], lambda row: att_in.at[row], f_send, f_recv, step, back
        )

    for step in (1, 2, 3):
        f_copy(step, False).start()
    att_in[at_y] = fin[at_y]
    for step in (1, 2, 3):
        f_copy(step, True).wait_recv()
    used = lax.broadcasted_iota(jnp.int32, (SLOTS, HEAD_DIM), 0) < count
    for g in range(GROUP):
        cols = slice(g * HEAD_DIM, (g + 1) * HEAD_DIM)
        att_o[0, :, cols] = jnp.where(used, att_in[g].astype(F32), 0.0).astype(BF16)

    gkv.finish()
    gq.finish()
    ring_kv.finish()
    for kind in range(4):
        ring_q.copy(kind, 0, 1).wait_send()
    hid_copy.wait_send()
    kv_part.wait_send()
    q_part.wait_send()
    for shift in (0, -1, 1, 2):
        to_sibling(shift, core).wait_send()
    for step in (1, 2, 3):
        sel_copy(step, False).wait_send()
        qy_copy(step, False).wait_send()
        f_copy(step, False).wait_send()
        for one in r_copy(step, False):
            one.wait_send()
    for one in (k_out, v_out):
        one.wait()


def shards(hidden_rows, w_query, w_key, w_value, cache_keys, cache_values, key_scale, value_scale, sel_index, sel_count):
    hbm_spec = pl.BlockSpec(memory_space=pltpu.HBM)
    dma = pltpu.SemaphoreType.DMA
    return pl.pallas_call(
        body,
        out_shape=(
            pltpu.VMEM((1, SLOTS, ROWS), BF16),
            pltpu.VMEM((1, SPAN_LEN, HEAD_DIM), BF16),
            pltpu.VMEM((1, SPAN_LEN, HEAD_DIM), BF16),
        ),
        in_specs=[hbm_spec] * 10,
        out_specs=(pl.BlockSpec(memory_space=pltpu.VMEM),) * 3,
        scratch_shapes=[
            pltpu.VMEM((CHIPS, 2 * SLOTS, DEPTH), BF16),
            pltpu.VMEM((CHIPS, DEPTH, 2 * HEAD_DIM), BF16),
            pltpu.VMEM((CHIPS, DEPTH, ROWS), BF16),
            pltpu.VMEM((2 * SLOTS, 2 * HEAD_DIM), F32),
            pltpu.VMEM((2 * SLOTS, ROWS), F32),
            pltpu.VMEM((SLOTS, 2 * HEAD_DIM), F32),
            pltpu.VMEM((SLOTS, ROWS), F32),
            pltpu.VMEM((2, SPAN_LEN, HEAD_DIM), BF16),
            pltpu.VMEM((SIDE, 2, 2, SPAN_LEN, HEAD_DIM), BF16),
            pltpu.VMEM((1, 1, SPAN_LEN), F32),
            pltpu.VMEM((1, 1, SPAN_LEN), F32),
            pltpu.VMEM((SIDE, 1, SLOTS), jnp.int32),
            pltpu.SMEM((1,), jnp.int32),
            pltpu.VMEM((GROUP, SLOTS, HEAD_DIM), BF16),
            pltpu.VMEM((SIDE, SIDE, SLOTS, HEAD_DIM), BF16),
            pltpu.VMEM((SIDE, ROWS, 128), F32),
            pltpu.VMEM((SIDE, ROWS, 128), F32),
            pltpu.VMEM((SIDE, ROWS, HEAD_DIM), F32),
            pltpu.VMEM((SIDE, ROWS, HEAD_DIM), BF16),
            pltpu.VMEM((SIDE, ROWS, HEAD_DIM), BF16),
            pltpu.VMEM((SIDE, 8, ROWS), F32),
            pltpu.VMEM((SIDE, 8, ROWS), F32),
            pltpu.VMEM((SIDE, SLOTS, HEAD_DIM), BF16),
            pltpu.VMEM((SIDE, SLOTS, HEAD_DIM), BF16),
            dma((10,)), dma((2,)), dma((2,)), dma((4,)), dma((4,)), dma((4,)),
            dma((40,)), dma((40,)), dma((40,)), dma((40,)), dma((4,)), dma((4,)), dma((4,)), dma((4,)),
            dma((3,)), dma((3,)), dma((3,)), dma((3,)), dma((3,)), dma((3,)), dma((3,)), dma((3,)), dma((3,)), dma((3,)),
        ],
        compiler_params=pltpu.CompilerParams(
            collective_id=0, has_side_effects=True, vmem_limit_bytes=63 * 1024 * 1024
        ),
        name="span_attention",
    )(hidden_rows, w_query, w_key, w_value, cache_keys, cache_values, key_scale, value_scale, sel_index, sel_count)


def solution(mesh):
    placed = (
        P(("req", "span"), None, None),
        P("span", "head"),
        P("span", "head"),
        P("span", "head"),
        P(("req", "span"), None, "head"),
        P(("req", "span"), None, "head"),
        P(("req", "span"), "head", None),
        P(("req", "span"), "head", None),
        P(("req", "span"), None),
        P(("req", "span")),
    )
    return jax.shard_map(
        shards,
        mesh=mesh,
        in_specs=placed,
        out_specs=(
            P(("req", "span"), None, "head"),
            P(("req", "span"), None, "head"),
            P(("req", "span"), None, "head"),
        ),
        check_vma=False,
    )
```

time: 128 us -> 97.7 us (0.76)
  the two profiles are of different devices: /device:TPU:63 before, /device:TPU:66 now
where the time goes in v2:
time: 97.7 us; the launch traced here: 97.4 us
  Pallas kernels  94.1 us (96%)
  local copies, waits for them, and re-layouts  2.06 us (2%)
  between operations  1.29 us (1%)
    pallas_call x1, Pallas kernels, shards(): pl.pallas_call(body, out_shape=(pltpu.VMEM((1, SLOTS, ROWS), BF16), pltpu...  94.1 us
    unnamed x3, local copies, waits for them, and re-layouts  2.06 us

profile of v2, /device:TPU:66, one launch (start us, length us, event | category | flops | bytes accessed | tf_op | source)
XLA Modules:
  0.0 97.4 jit_solution(14053494878137555039)
XLA Ops:
  1.3 94.1 %span_attention.1 = (bf16[1,128,512]{2,1,0:T(8,128)(2,1)S(1)}, bf16[1,1024,128]{2,1,0:T(8,128)(2,1)S(1)}, bf16[1,1024,128]{2,1,0:T(8,128)(2,1)S(1)}) custom-call(bf16[1,128,8192]{2,1,0:T(8,128)(2,1)} %hid.1, bf16[256,512]{1,0:T(8,128)(2,1)} %wq.1, bf16[256,128]{1,0:T(8,128)(2,1)} %wk.1, bf16[256,128]{1,0:T(8,128)(2,1)} %wv.1, bf16[1,1024,128]{2,1,0:T(8,128)(2,1)} %ck.1, ...), custom_call_target="tpu_custom_call" | custom-call | tf_op jit(solution)/shard_map/span_attention/pallas_call | solution.py:529
  95.4 0.7 copy.16
  96.0 0.7 copy.17
  96.7 0.7 copy.18

commit v3 on v2

--- a/solution.py
+++ b/solution.py
@@ -1,3 +1,4 @@
+import functools
 import math
 
 import jax
@@ -166,28 +167,36 @@
     acc[...] = part if first else acc[...] + part
 
 
-def run_gather(gather, acc, hid_v, buf, first_work, late_work, last_work):
+def run_gather(gather, acc, hid_v, buf, **hooks):
+    def hook(name):
+        if name in hooks:
+            hooks[name]()
+
     def work(*pairs):
         for dx, dy in pairs:
             project(acc, hid_v, buf, gather.block(dx, dy))
 
-    first_work()
+    hook("start")
     gather.fulls(1, 0)
+    hook("one")
     gather.fulls(2, 0)
+    hook("two")
     work((-1, 0), (1, 0), (0, -1), (0, 1))
     gather.quarters(1, 0)
     gather.fulls(2, 1)
+    hook("three")
     gather.fulls(2, 2)
+    hook("four")
     work((-1, -1), (1, -1), (-1, 1), (1, 1))
     gather.quarters(2, 0)
     work((2, 0), (0, 2))
-    late_work()
+    hook("five")
     gather.fulls(2, 3)
     gather.quarters(2, 1)
     gather.quarters(2, 2)
     work((2, -1), (2, 1), (-1, 2), (1, 2))
     gather.quarters(2, 3)
-    last_work()
+    hook("six")
     work((2, 2))
 
 
@@ -257,7 +266,6 @@
     loads[1].wait()
     gkv.begin()
     loads[2].wait()
-    gq.begin()
 
     def send_hidden(block, carry):
         start = pl.multiple_of((block * 2 + 1 - core) * DEPTH, DEPTH)
@@ -301,7 +309,7 @@
         project(acc_kv, hid_v, wkv_buf, chip, first=True)
         project(acc_q, hid_v, wq_buf, chip, first=True)
 
-    run_gather(gkv, acc_kv, hid_v, wkv_buf, first_kv, lambda: None, lambda: None)
+    run_gather(gkv, acc_kv, hid_v, wkv_buf, start=first_kv, six=gq.begin)
     kv_part = remote(
         acc_kv.at[pl.ds(SLOTS, SLOTS), :], pkv_in, part_sem.at[0], part_sem.at[1], sibling
     )
@@ -310,19 +318,22 @@
     slot_row = lax.broadcasted_iota(jnp.int32, (1, SLOTS), 1)
     wanted = jnp.where(slot_row < count, sel[at_y], -1)
 
-    ring_kv = Ring(
-        lambda row, which: kv.at[row, which, core], lambda row: kv.at[row, :, core],
-        at_y, in_column, ring_kv_send, ring_kv_recv,
-    )
+    rings = [
+        Ring(
+            lambda row, half, which=which: kv.at[row, which, core, pl.ds(half * 512, 512)],
+            lambda row, which=which: kv.at[row, which, core],
+            at_y, in_column, ring_kv_send.at[which], ring_kv_recv.at[which],
+        )
+        for which in (0, 1)
+    ]
     ring_q = Ring(
         lambda x, which: qbuf.at[x, pl.ds(which * 2, 2)], lambda x: qbuf.at[x],
         at_x, in_row, ring_q_send, ring_q_recv,
     )
 
-    def to_sibling(shift, owner):
-        block = ring_kv.place(shift)
-        ref = kv.at[block, :, owner]
-        return remote(ref, ref, sib_send.at[shift + 1], sib_recv.at[shift + 1], sibling)
+    def to_sibling(which, shift, owner):
+        ref = kv.at[rings[which].place(shift), which, owner]
+        return remote(ref, ref, sib_send.at[which, shift + 1], sib_recv.at[which, shift + 1], sibling)
 
     k_out = pltpu.make_async_copy(kv.at[at_y, 0, core], bk_o.at[0], out_sem.at[0])
     v_out = pltpu.make_async_copy(kv.at[at_y, 1, core], bv_o.at[0], out_sem.at[1])
@@ -332,34 +343,36 @@
         fresh = (acc_kv[0:SLOTS, :] + pkv_in[...]).astype(BF16)
         ones = jnp.ones((SLOTS, HEAD_DIM), BF16)
 
-        def part(step, carry):
-            start = pl.multiple_of(step * 128, 128)
-            rows = lax.broadcasted_iota(jnp.int32, (128, SLOTS), 0) + start
+        for step in range(SPAN_LEN // 128):
+            here = slice(step * 128, (step + 1) * 128)
+            rows = lax.broadcasted_iota(jnp.int32, (128, SLOTS), 0) + step * 128
             chosen = jnp.where(rows == wanted, 1.0, 0.0).astype(BF16)
             moved = jnp.dot(chosen, fresh, preferred_element_type=F32)
             hit = jnp.dot(chosen, ones, preferred_element_type=F32) > 0.5
             for which in (0, 1):
                 new = moved[:, which * HEAD_DIM:(which + 1) * HEAD_DIM]
-                old = kv[at_y, which, core, pl.ds(start, 128), :].astype(F32)
-                kv[at_y, which, core, pl.ds(start, 128), :] = jnp.where(hit, new, old).astype(BF16)
-            return carry
-
-        lax.fori_loop(0, SPAN_LEN // 128, part, 0)
-        ring_kv.begin()
-        to_sibling(0, core).start()
+                old = kv[at_y, which, core, here, :].astype(F32)
+                kv[at_y, which, core, here, :] = jnp.where(hit, new, old).astype(BF16)
+
+        for which in (0, 1):
+            rings[which].begin()
+        for which in (0, 1):
+            to_sibling(which, 0, core).start()
         k_out.start()
         v_out.start()
 
-    def pass_kv():
+    def pass_on(which):
         for kind, shift in ((0, -1), (1, 1)):
-            ring_kv.full(kind)
-            to_sibling(shift, core).start()
-
-    def end_kv():
-        ring_kv.halves()
-        to_sibling(2, core).start()
-
-    run_gather(gq, acc_q, hid_v, wq_buf, blend, pass_kv, end_kv)
+            rings[which].full(kind)
+            to_sibling(which, shift, core).start()
+
+    def end(which):
+        rings[which].halves()
+        to_sibling(which, 2, core).start()
+
+    pass_k, pass_v = functools.partial(pass_on, 0), functools.partial(pass_on, 1)
+    end_k, end_v = functools.partial(end, 0), functools.partial(end, 1)
+    run_gather(gq, acc_q, hid_v, wq_buf, start=blend, two=pass_k, three=pass_v, five=end_k, six=end_v)
     q_part = remote(acc_q.at[pl.ds(SLOTS, SLOTS), :], pq_in, part_sem.at[2], part_sem.at[3], sibling)
     q_part.start()
     peak[...] = jnp.full((SIDE, ROWS, 128), -1e30, F32)
@@ -379,7 +392,8 @@
         qy_copy(step, False).start()
     qbuf[at_x, at_y] = q_stage[at_y]
     for shift in (0, -1, 1, 2):
-        to_sibling(shift, 1 - core).wait_recv()
+        for which in (0, 1):
+            to_sibling(which, shift, 1 - core).wait_recv()
     for step in (1, 2, 3):
         qy_copy(step, True).wait_recv()
         sel_copy(step, True).wait_recv()
@@ -505,14 +519,16 @@
 
     gkv.finish()
     gq.finish()
-    ring_kv.finish()
+    for one in rings:
+        one.finish()
     for kind in range(4):
         ring_q.copy(kind, 0, 1).wait_send()
     hid_copy.wait_send()
     kv_part.wait_send()
     q_part.wait_send()
     for shift in (0, -1, 1, 2):
-        to_sibling(shift, core).wait_send()
+        for which in (0, 1):
+            to_sibling(which, shift, core).wait_send()
     for step in (1, 2, 3):
         sel_copy(step, False).wait_send()
         qy_copy(step, False).wait_send()
@@ -560,8 +576,8 @@
             pltpu.VMEM((SIDE, 8, ROWS), F32),
             pltpu.VMEM((SIDE, SLOTS, HEAD_DIM), BF16),
             pltpu.VMEM((SIDE, SLOTS, HEAD_DIM), BF16),
-            dma((10,)), dma((2,)), dma((2,)), dma((4,)), dma((4,)), dma((4,)),
-            dma((40,)), dma((40,)), dma((40,)), dma((40,)), dma((4,)), dma((4,)), dma((4,)), dma((4,)),
+            dma((10,)), dma((2,)), dma((2,)), dma((4,)), dma((2, 4)), dma((2, 4)),
+            dma((40,)), dma((40,)), dma((40,)), dma((40,)), dma((2, 4)), dma((2, 4)), dma((4,)), dma((4,)),
             dma((3,)), dma((3,)), dma((3,)), dma((3,)), dma((3,)), dma((3,)), dma((3,)), dma((3,)), dma((3,)), dma((3,)),
         ],
         compiler_params=pltpu.CompilerParams(

time: 97.7 us -> 95.2 us (0.974)
  Pallas kernels: 94.1 us -> 91.8 us
    pallas_call x1, Pallas kernels: 94.1 us -> 91.8 us  [shards(): pl.pallas_call(body, out_shape=(pltpu.VMEM((1, SLOTS, ROWS), BF16), pltpu...]
where the time goes in v3:
time: 95.2 us; the launch traced here: 95.1 us
  Pallas kernels  91.8 us (96%)
  local copies, waits for them, and re-layouts  2.06 us (2%)
  between operations  1.29 us (1%)
    pallas_call x1, Pallas kernels, shards(): pl.pallas_call(body, out_shape=(pltpu.VMEM((1, SLOTS, ROWS), BF16), pltpu...  91.8 us
    unnamed x3, local copies, waits for them, and re-layouts  2.06 us

profile of v3, /device:TPU:66, one launch (start us, length us, event | category | flops | bytes accessed | tf_op | source)
XLA Modules:
  0.0 95.1 jit_solution(14578356017635829034)
XLA Ops:
  1.3 91.8 %span_attention.1 = (bf16[1,128,512]{2,1,0:T(8,128)(2,1)S(1)}, bf16[1,1024,128]{2,1,0:T(8,128)(2,1)S(1)}, bf16[1,1024,128]{2,1,0:T(8,128)(2,1)S(1)}) custom-call(bf16[1,128,8192]{2,1,0:T(8,128)(2,1)} %hid.1, bf16[256,512]{1,0:T(8,128)(2,1)} %wq.1, bf16[256,128]{1,0:T(8,128)(2,1)} %wk.1, bf16[256,128]{1,0:T(8,128)(2,1)} %wv.1, bf16[1,1024,128]{2,1,0:T(8,128)(2,1)} %ck.1, ...), custom_call_target="tpu_custom_call" | custom-call | tf_op jit(solution)/shard_map/span_attention/pallas_call | solution.py:545
  93.0 0.7 copy.16
  93.7 0.7 copy.17
  94.4 0.7 copy.18

commit v4 on v3

--- a/solution.py
+++ b/solution.py
@@ -391,13 +391,13 @@
     for step in (1, 2, 3):
         qy_copy(step, False).start()
     qbuf[at_x, at_y] = q_stage[at_y]
-    for shift in (0, -1, 1, 2):
-        for which in (0, 1):
-            to_sibling(which, shift, 1 - core).wait_recv()
     for step in (1, 2, 3):
         qy_copy(step, True).wait_recv()
         sel_copy(step, True).wait_recv()
     ring_q.begin()
+    for shift in (0, -1, 1, 2):
+        for which in (0, 1):
+            to_sibling(which, shift, 1 - core).wait_recv()
 
     def scored(x, row, block):
         keys = kv[block, 0].reshape(KEYS, HEAD_DIM)
@@ -449,18 +449,15 @@
         return jnp.transpose(both)[0:8, :]
 
     def one_chip(index, carry):
-        step = jnp.where(index == 0, 0, jnp.where(index == 1, 3, jnp.where(index == 2, 1, 2)))
+        step = jnp.where(index == 0, 0, jnp.where(index == 1, 3, jnp.where(index == 2, 2, 1)))
         x = lax.rem(at_x + step, SIDE)
 
         @pl.when(index == 1)
         def _():
             ring_q.full(0)
+            ring_q.full(1)
 
         @pl.when(index == 2)
-        def _():
-            ring_q.full(1)
-
-        @pl.when(index == 3)
         def _():
             ring_q.halves()
 
@@ -475,7 +472,7 @@
             r_out[x] = accum[x].astype(BF16)
             s_out[x] = stats(x)
 
-        for which, way in ((1, 3), (2, 1), (3, 2)):
+        for which, way in ((1, 3), (2, 2), (3, 1)):
             @pl.when(index == which)
             def _(way=way):
                 for one in r_copy(way, False):

time: 95.2 us -> 94.5 us (level)
  no operation moved by 1% of the time
where the time goes in v4:
time: 94.5 us; the launch traced here: 94.4 us
  Pallas kernels  91.1 us (96%)
  local copies, waits for them, and re-layouts  2.06 us (2%)
  between operations  1.29 us (1%)
    pallas_call x1, Pallas kernels, shards(): pl.pallas_call(body, out_shape=(pltpu.VMEM((1, SLOTS, ROWS), BF16), pltpu...  91.1 us
    unnamed x3, local copies, waits for them, and re-layouts  2.06 us

profile of v4, /device:TPU:66, one launch (start us, length us, event | category | flops | bytes accessed | tf_op | source)
XLA Modules:
  0.0 94.4 jit_solution(3295938535295311852)
XLA Ops:
  1.3 91.1 %span_attention.1 = (bf16[1,128,512]{2,1,0:T(8,128)(2,1)S(1)}, bf16[1,1024,128]{2,1,0:T(8,128)(2,1)S(1)}, bf16[1,1024,128]{2,1,0:T(8,128)(2,1)S(1)}) custom-call(bf16[1,128,8192]{2,1,0:T(8,128)(2,1)} %hid.1, bf16[256,512]{1,0:T(8,128)(2,1)} %wq.1, bf16[256,128]{1,0:T(8,128)(2,1)} %wk.1, bf16[256,128]{1,0:T(8,128)(2,1)} %wv.1, bf16[1,1024,128]{2,1,0:T(8,128)(2,1)} %ck.1, ...), custom_call_target="tpu_custom_call" | custom-call | tf_op jit(solution)/shard_map/span_attention/pallas_call | solution.py:542
  92.4 0.7 copy.16
  93.0 0.7 copy.17
  93.7 0.7 copy.18

commit v5 on v4

--- a/solution.py
+++ b/solution.py
@@ -297,11 +297,12 @@
     for step in (1, 2, 3):
         sel_copy(step, False).start()
 
-    for which, scale in enumerate((ks, vs)):
-        for part in range(SPAN_LEN // 128):
-            rows = slice(part * 128, (part + 1) * 128)
-            spread = jnp.transpose(jnp.broadcast_to(scale[0, :, rows], (128, 128)))
-            kv[at_y, which, core, rows, :] = (cache_v[which, rows, :].astype(F32) * spread).astype(BF16)
+    def dequantize():
+        for which, scale in enumerate((ks, vs)):
+            for part in range(SPAN_LEN // 128):
+                rows = slice(part * 128, (part + 1) * 128)
+                spread = jnp.transpose(jnp.broadcast_to(scale[0, :, rows], (128, 128)))
+                kv[at_y, which, core, rows, :] = (cache_v[which, rows, :].astype(F32) * spread).astype(BF16)
 
     def first_kv():
         pltpu.make_async_copy(hid_own, hid_own, local_sem.at[5]).wait()
@@ -309,7 +310,7 @@
         project(acc_kv, hid_v, wkv_buf, chip, first=True)
         project(acc_q, hid_v, wq_buf, chip, first=True)
 
-    run_gather(gkv, acc_kv, hid_v, wkv_buf, start=first_kv, six=gq.begin)
+    run_gather(gkv, acc_kv, hid_v, wkv_buf, two=first_kv, four=dequantize, six=gq.begin)
     kv_part = remote(
         acc_kv.at[pl.ds(SLOTS, SLOTS), :], pkv_in, part_sem.at[0], part_sem.at[1], sibling
     )

time: 94.5 us -> 94.1 us (level)
  no operation moved by 1% of the time
where the time goes in v5:
time: 94.1 us; the launch traced here: 94 us
  Pallas kernels  90.7 us (96%)
  local copies, waits for them, and re-layouts  2.06 us (2%)
  between operations  1.29 us (1%)
    pallas_call x1, Pallas kernels, shards(): pl.pallas_call(body, out_shape=(pltpu.VMEM((1, SLOTS, ROWS), BF16), pltpu...  90.7 us
    unnamed x3, local copies, waits for them, and re-layouts  2.06 us

profile of v5, /device:TPU:66, one launch (start us, length us, event | category | flops | bytes accessed | tf_op | source)
XLA Modules:
  0.0 94.0 jit_solution(11303953986918015147)
XLA Ops:
  1.3 90.7 %span_attention.1 = (bf16[1,128,512]{2,1,0:T(8,128)(2,1)S(1)}, bf16[1,1024,128]{2,1,0:T(8,128)(2,1)S(1)}, bf16[1,1024,128]{2,1,0:T(8,128)(2,1)S(1)}) custom-call(bf16[1,128,8192]{2,1,0:T(8,128)(2,1)} %hid.1, bf16[256,512]{1,0:T(8,128)(2,1)} %wq.1, bf16[256,128]{1,0:T(8,128)(2,1)} %wk.1, bf16[256,128]{1,0:T(8,128)(2,1)} %wv.1, bf16[1,1024,128]{2,1,0:T(8,128)(2,1)} %ck.1, ...), custom_call_target="tpu_custom_call" | custom-call | tf_op jit(solution)/shard_map/span_attention/pallas_call | solution.py:543
  91.9 0.7 copy.16
  92.6 0.7 copy.17
  93.3 0.7 copy.18
